TPU v7x, 32 devices: a whole 2x2x4 slice. The times are simulated.
32 devices in a mesh: freq: 8 (over z, x), pair: 4 (over y, core).
Axes of the slice: x: 2, y: 2, z: 4, core: 2. Of those that a mesh axis runs over, the one named last changes fastest.
Arguments:
- voltages: int32 [2048, 103, 2048], P(('pair', 'freq')), may hold values from -8 to 7
- gains: float32 [2048, 24], P(('pair', 'freq')), may hold values from 0.3 to 3
Outputs:
- visibilities: bfloat16 [24, 2, 2048, 2048], P('freq', None, 'pair')
All inputs are finite; a program needn't handle non-finite values.
Results may differ from a plain program's by a relative error of at most 0.0078.
Values may be sent and summed in bfloat16 or wider, within the bound.
No kernel may reach another device: no remote copies, remote signals or barrier semaphores. Data moves between devices by JAX's collectives and lax.ppermute only.
A program may use at most 192 MiB of HBM per device.

v0:
```python
import math

import jax
import jax.numpy as jnp
from jax import lax
from jax.sharding import PartitionSpec as P

NFFT = 2048
TAPS = 8
SAMPLES = 96
FIRST = 256


def filter_table():
    positions = jnp.arange(TAPS * NFFT, dtype=jnp.float32)
    span_width = float(TAPS * NFFT)
    window = 0.5 - 0.5 * jnp.cos(2.0 * jnp.pi * (positions + 0.5) / span_width)
    taps_table = window * jnp.sinc((positions - span_width / 2 + 0.5) / NFFT)
    return taps_table.reshape(TAPS, NFFT)


def dft_table(first_bin, count):
    samples = jnp.arange(NFFT, dtype=jnp.int32)
    bin_index = first_bin + jnp.arange(count, dtype=jnp.int32)
    phases = bin_index[:, None] * samples[None, :] % NFFT
    angles = phases.astype(jnp.float32) * (2.0 * math.pi / NFFT)
    amplitude = 0.25 / math.sqrt(NFFT)
    cos_rows = (jnp.cos(angles) * amplitude).astype(jnp.bfloat16)
    sin_rows = (-jnp.sin(angles) * amplitude).astype(jnp.bfloat16)
    return (cos_rows, sin_rows)


def correlate(row_side, col_side):
    row_real, row_imag = (row_side[0], row_side[1])
    col_real, col_imag = (col_side[0], col_side[1])

    def contract(left_side, right_side):
        return jnp.einsum("csr,csk->crk", left_side, right_side, preferred_element_type=jnp.float32)

    real_sum = contract(row_real, col_real) + contract(row_imag, col_imag)
    imag_sum = contract(row_imag, col_real) - contract(row_real, col_imag)
    result = jnp.stack([real_sum, imag_sum], axis=1)
    return (result * (1.0 / SAMPLES)).astype(jnp.bfloat16)


def body(voltages, gains):
    n_freq = lax.axis_size("freq")
    local_inputs = voltages.shape[0]
    all_channels = gains.shape[1]
    ch_dev = all_channels // n_freq
    taps_table = filter_table()
    as_float = voltages.astype(jnp.float32)
    filtered = taps_table[0] * as_float[:, 0:SAMPLES, :]
    for tap_index in range(1, TAPS):
        filtered = (
            filtered + taps_table[tap_index] * as_float[:, tap_index : tap_index + SAMPLES, :]
        )
    filtered = filtered.astype(jnp.bfloat16).reshape(local_inputs * SAMPLES, NFFT)
    cos_rows, sin_rows = dft_table(FIRST, all_channels)
    dft_rows = jnp.stack(
        [cos_rows.reshape(n_freq, ch_dev, NFFT), sin_rows.reshape(n_freq, ch_dev, NFFT)], 1
    )
    dft_rows = dft_rows.reshape(2 * all_channels, NFFT)
    spectra = lax.dot_general(
        dft_rows, filtered, (((1,), (1,)), ((), ())), preferred_element_type=jnp.float32
    )
    gain_rows = jnp.broadcast_to(
        gains.T.reshape(n_freq, 1, ch_dev, local_inputs), (n_freq, 2, ch_dev, local_inputs)
    )
    gain_rows = gain_rows.reshape(2 * all_channels, local_inputs, 1)
    spectra = spectra.reshape(2 * all_channels, local_inputs, SAMPLES) * gain_rows
    spectra = spectra.astype(jnp.bfloat16).reshape(2 * all_channels, local_inputs * SAMPLES)
    turned = lax.all_to_all(spectra, "freq", split_axis=0, concat_axis=1, tiled=True)
    row_side = turned.reshape(2, ch_dev, n_freq * local_inputs, SAMPLES).transpose(0, 1, 3, 2)
    return correlate(row_side, lax.all_gather(row_side, "pair", axis=3, tiled=True))


def solution(mesh):
    placed = (P(("pair", "freq"), None, None), P(("pair", "freq"), None))
    return jax.shard_map(
        body, mesh=mesh, in_specs=placed, out_specs=P("freq", None, "pair", None), check_vma=False
    )
```

profile of v0, /device:TPU:0, one launch (start us, length us, event | category | flops | bytes accessed | tf_op | source)
XLA Modules:
  0.0 311.9 jit_solution(2435064820251217059)
XLA Ops:
  6.5 0.0 all-gather.2.cloned.1.call-start
  6.5 0.3 fusion.25
  6.9 0.0 copy-start.2
  6.9 36.1 %convert_element_type.56 = f32[64,103,2048]{2,0,1:T(8,128)} convert(s32[64,103,2048]{2,0,1:T(8,128)} %param.2) | non-fusion elementwise | flops 13500416 | bytes 108003328 | tf_op jit(solution)/shard_map/convert_element_type | solution.py:52
  43.0 0.9 multiply_convert_fusion.2
  43.9 0.2 copy.12
  44.1 0.2 reshape.137
  44.3 0.0 copy-done.2
  44.3 0.1 copy.14
  44.4 131.0 %fusion.1 = bf16[64,96,2048]{2,0,1:T(8,128)(2,1)} fusion(f32[64,103,2048]{2,0,1:T(8,128)} %convert_element_type.56, f32[2048]{0:T(1024)S(1)} %get-tuple-element.6, f32[2048]{0:T(1024)S(1)} %get-tuple-element.7, f32[2048]{0:T(1024)S(1)} %get-tuple-element.8, f32[2048]{0:T(1024)S(1)} %get-tuple-element.9, f32[2048]{0:T(1024)S(1)} %get-tuple-element.10, ...), kind=kLoop, calls=%fused_computation.2 | loop fusion | flops 201326592 | bytes 427884544 | tf_op jit(solution)/shard_map/convert_element_type | solution.py:58
  175.4 41.0 %multiply_convert_fusion = bf16[48,64,96]{2,0,1:T(8,128)(2,1)S(1)} fusion(bf16[48,2048,1]{1,0,2:T(8,128)(2,1)S(1)} %reshape.137, bf16[64,96,2048]{2,0,1:T(8,128)(2,1)} %fusion.1, f32[48,64]{0,1:T(8,128)S(1)} %copy.14), kind=kOutput, calls=%fused_computation.22 | convolution fusion | flops 1208549376 | bytes 25964544 | tf_op jit(solution)/shard_map/dot_general | solution.py:64
  216.4 0.2 copy.15
  216.6 1.1 all_to_all.12
  217.7 27.2 %all_to_all.16 = bf16[8,6,6144]{2,1,0:T(8,128)(2,1)S(1)} all-to-all(bf16[8,6,6144]{2,1,0:T(8,128)(2,1)S(1)} %all_to_all.12), channel_id=1, replica_groups=mesh['freq'=8,'pair'=4] {'freq'}, dimensions={0} | all-to-all | bytes 1179648 | tf_op jit(solution)/shard_map/all_to_all | solution.py:73
  244.9 0.3 copy.16
  245.2 0.8 reshape.136
  246.0 1.1 copy.17
  247.1 0.0 copy-start.1
  247.1 0.0 all-gather.2.cloned.1.call-update
  247.1 23.3 %all-gather.2.cloned.1.call-done = bf16[2,3,96,2048]{3,2,1,0:T(8,128)(2,1)} async-done(((bf16[2,3,96,512]{3,2,1,0:T(8,128)(2,1)}), bf16[2,3,96,2048]{3,2,1,0:T(8,128)(2,1)}) %all-gather.2.cloned.1.call-update) | async-done | bytes 2359312 | tf_op jit(solution)/shard_map/all_gather | solution.py:75
  270.4 3.2 %fusion.14 = f32[3,512,2048]{2,1,0:T(8,128)S(1)} fusion(bf16[2,3,96,2048]{3,2,1,0:T(8,128)(2,1)} %all-gather.2.cloned.1.call-done, bf16[2,3,96,512]{3,2,1,0:T(8,128)(2,1)} %bitcast.25), kind=kOutput, calls=%fused_computation.26 | convolution fusion | flops 603979776 | bytes 14057472 | tf_op jit(solution)/shard_map/csr,csk->crk/dot_general | solution.py:38
  273.6 3.2 %fusion.13 = f32[3,512,2048]{2,1,0:T(8,128)S(1)} fusion(bf16[2,3,96,2048]{3,2,1,0:T(8,128)(2,1)} %all-gather.2.cloned.1.call-done, bf16[2,3,96,512]{3,2,1,0:T(8,128)(2,1)} %bitcast.26), kind=kOutput, calls=%fused_computation.25 | convolution fusion | flops 603979776 | bytes 14057472 | tf_op jit(solution)/shard_map/csr,csk->crk/dot_general | solution.py:38
  276.8 0.0 copy-done.1
  276.8 7.6 %add_bitcast_fusion = f32[3,1,512,2048]{3,2,0,1:T(8,128)} fusion(f32[3,512,2048]{2,1,0:T(8,128)S(1)} %fusion.14, bf16[2,3,96,2048]{3,2,1,0:T(8,128)(2,1)} %all-gather.2.cloned.1.call-done, bf16[2,3,96,512]{3,2,1,0:T(8,128)(2,1)S(1)} %bitcast.27), kind=kOutput, calls=%fused_computation.21 | convolution fusion | flops 607125504 | bytes 26640384 | tf_op jit(solution)/shard_map/csr,csk->crk/dot_general | solution.py:38
  284.5 0.0 copy-start
  284.5 8.2 %subtract_bitcast_fusion = f32[3,1,512,2048]{3,2,0,1:T(8,128)} fusion(f32[3,512,2048]{2,1,0:T(8,128)S(1)} %fusion.13, bf16[2,3,96,2048]{3,2,1,0:T(8,128)(2,1)} %all-gather.2.cloned.1.call-done, bf16[2,3,96,512]{3,2,1,0:T(8,128)(2,1)S(1)} %bitcast.28), kind=kOutput, calls=%fused_computation.20 | convolution fusion | flops 607125504 | bytes 26640384 | tf_op jit(solution)/shard_map/csr,csk->crk/dot_general | solution.py:38
  292.7 0.0 copy-done
  292.7 7.3 %fusion.8 = bf16[3,2,512,2048]{3,2,0,1:T(8,128)(2,1)S(1)} fusion(f32[3,1,512,2048]{3,2,0,1:T(8,128)} %subtract_bitcast_fusion, f32[3,1,512,2048]{3,2,0,1:T(8,128)S(1)} %copy-done), kind=kLoop, calls=%fused_computation.17 | loop fusion | flops 18874368 | bytes 37748736 | tf_op jit(solution)/shard_map/convert_element_type | solution.py:43
  300.0 5.1 %copy.18 = bf16[3,2,512,2048]{3,2,1,0:T(8,128)(2,1)} copy(bf16[3,2,512,2048]{3,2,0,1:T(8,128)(2,1)S(1)} %fusion.8) | data formatting | bytes 25165824 | tf_op jit(solution)/shard_map/convert_element_type | solution.py:43
  (6 shorter events, 0.1 us)
Async XLA Ops:
  6.5 263.9 %all-gather.2.cloned.1.call-start = ((), (), s32[]{:S(2)}) async-start(), calls=%async_computation.1 | async-start | bytes 2949120 | tf_op jit(solution)/shard_map/all_gather | solution.py:75
  6.9 37.4 %copy-start.2 = (f32[64,24]{0,1:T(8,128)S(1)}, f32[64,24]{0,1:T(8,128)}, u32[]{:S(2)}) copy-start(f32[64,24]{0,1:T(8,128)} %param.3) | copy-start | bytes 18436
  247.1 29.7 %copy-start.1 = (bf16[2,3,512,96]{2,3,1,0:T(8,128)(2,1)S(1)}, bf16[2,3,512,96]{2,3,1,0:T(8,128)(2,1)}, u32[]{:S(2)}) copy-start(bf16[2,3,512,96]{2,3,1,0:T(8,128)(2,1)} %copy.17) | copy-start | bytes 1769476
  284.5 8.2 %copy-start = (f32[3,1,512,2048]{3,2,0,1:T(8,128)S(1)}, f32[3,1,512,2048]{3,2,0,1:T(8,128)}, u32[]{:S(2)}) copy-start(f32[3,1,512,2048]{3,2,0,1:T(8,128)} %add_bitcast_fusion) | copy-start | bytes 37748740
Sparse Core Ops, SparseCore 0:
  247.3 23.0 all-gather.1
where the time goes:
time: 312 us
  other arithmetic  176 us (56%)
  matrix products  63.2 us (20%)
  blocking collectives  27.2 us (9%)
  waiting for transfers between devices  23.3 us (7%)
  between operations  13.5 us (4%)
  local copies, waits for them, and re-layouts  9.09 us (3%)
    convert_element_type x1, other arithmetic, body(): filtered.astype(jnp.bfloat16).reshape(local_inputs * SAMPLES, NFFT)  131 us
    dot_general x1, matrix products, body(): lax.dot_general(dft_rows, filtered, (((1,), (1,)), ((), ())), preferred_e...  41 us
    convert_element_type x1, other arithmetic, body(): as_float = voltages.astype(jnp.float32)  36.1 us
    all_to_all x1, blocking collectives, body(): lax.all_to_all(spectra, 'freq', split_axis=0, concat_axis=1, tiled=True)  27.2 us
    all_gather x1, waiting for transfers between devices, body(): lax.all_gather(row_side, 'pair', axis=3, tiled=True)  23.3 us
    dot_general x4, matrix products, contract(): jnp.einsum('csr,csk->crk', left_side, right_side, preferred_element_type=...  22.3 us
    convert_element_type x1, other arithmetic, correlate(): return (result * (1.0 / SAMPLES)).astype(jnp.bfloat16)  7.3 us
  transfers between devices with their start and end apart: 1, of which 1 were waited for; matrix products, arithmetic and copies ran while one was open for 0% of the time, Pallas kernels for 0%

commit v1 on v0

v1 whole, which is shorter than its diff:
```python
import functools
import math

import jax
import jax.numpy as jnp
import numpy as np
from jax import lax
from jax.experimental import pallas as pl
from jax.experimental.pallas import tpu as pltpu
from jax.sharding import PartitionSpec as P

NFFT = 2048
TAPS = 8
SAMPLES = 96
FIRST = 256
LANES = 128
VMEM_LIMIT = 36 * 1024 * 1024


def tables(channels):
    j = np.arange(TAPS * NFFT, dtype=np.float64)
    window = 0.5 - 0.5 * np.cos(2.0 * np.pi * (j + 0.5) / (TAPS * NFFT))
    taps = (window * np.sinc((j - TAPS * NFFT / 2 + 0.5) / NFFT)).astype(np.float32)
    bins = FIRST + np.arange(channels)
    angles = (bins[:, None] * np.arange(NFFT)[None, :] % NFFT) * (2.0 * math.pi / NFFT)
    amplitude = 0.25 / math.sqrt(NFFT)
    rows = np.stack([np.cos(angles) * amplitude, -np.sin(angles) * amplitude], 1)
    rows = rows.astype(np.float32).astype(jnp.bfloat16).astype(np.float32)
    return taps.reshape(TAPS, NFFT), rows.reshape(2 * channels, NFFT)


def channelize_kernel(rows, n_freq, x_hbm, tap_hbm, dft_hbm, gain_hbm, *refs):
    outs, refs = refs[:n_freq], refs[n_freq:]
    xs, ws, taps, dft, gains, carry, scale, sums, x_sem, sem = refs
    lanes = xs.shape[1]
    per_frame = lanes // TAPS
    tiles = lanes // LANES
    ahead = xs.shape[0] - 1
    piece = lanes // x_sem.shape[1]
    full, rest = divmod(x_hbm.shape[0], lanes)

    def copies(block, size):
        slot = lax.rem(block, xs.shape[0])
        found = []
        for k in range(x_sem.shape[1]):
            count = min(piece, size - k * piece)
            if count > 0:
                start = pl.multiple_of(block * lanes + k * piece, 16)
                found.append(
                    pltpu.make_async_copy(
                        x_hbm.at[pl.ds(start, count)],
                        xs.at[slot, pl.ds(k * piece, count)],
                        x_sem.at[slot, k],
                    )
                )
        return found

    def fetch(block):
        @pl.when(block < full)
        def _():
            for copy in copies(block, lanes):
                copy.start()

        if rest:

            @pl.when(block == full)
            def _():
                for copy in copies(block, rest):
                    copy.start()

    def block_of(block, size):
        for copy in copies(block, size):
            copy.wait()
        fetch(block + ahead)
        slot = lax.rem(block, xs.shape[0])
        part = min(256, lanes)
        pieces = []
        for at in range(0, lanes, part):
            x = xs[slot, at : at + part].astype(jnp.bfloat16)
            pieces.append(
                lax.dot_general(
                    ws[...], x, (((1,), (1,)), ((), ())), preferred_element_type=jnp.float32
                )
            )
        y = jnp.concatenate(pieces, axis=1)
        lane = lax.broadcasted_iota(jnp.int32, (rows, lanes), 1)
        low = y[0:rows]
        high = carry[...]
        for tap in range(1, TAPS):
            turned = pltpu.roll(y[tap * rows : (tap + 1) * rows], lanes - tap * per_frame, 1)
            keep = lane < lanes - tap * per_frame
            low = low + jnp.where(keep, turned, 0.0)
            high = high + jnp.where(keep, 0.0, turned)
        carry[...] = low
        for tile in range(tiles):
            sums[:, block * tiles + 8 - tiles + tile, :] = (
                high[:, tile * LANES : (tile + 1) * LANES] * scale[...]
            )

    small = [
        pltpu.make_async_copy(source, target, sem.at[k])
        for k, (source, target) in enumerate([(tap_hbm, taps), (dft_hbm, dft), (gain_hbm, gains)])
    ]
    for copy in small + copies(0, lanes):
        copy.start()
    row = lax.broadcasted_iota(jnp.int32, (rows, rows // 2), 0)
    column = lax.broadcasted_iota(jnp.int32, (rows, rows // 2), 1)
    spread = jnp.where(row // 2 == column, 1.0, 0.0).astype(jnp.float32)
    for copy in small:
        copy.wait()
    for tap in range(TAPS):
        ws[tap * rows : (tap + 1) * rows] = (taps[tap : tap + 1] * dft[...]).astype(jnp.bfloat16)
    for block in range(1, ahead):
        for copy in copies(block, lanes):
            copy.start()
    each = jnp.dot(
        spread,
        gains[...],
        precision=lax.Precision.HIGHEST,
        preferred_element_type=jnp.float32,
    )
    scale[...] = jnp.concatenate([each] * (LANES // per_frame), axis=1)
    carry[...] = jnp.zeros_like(carry)

    @pl.loop(0, full)
    def _(block):
        block_of(block, lanes)

    if rest:
        block_of(full, rest)
    share = rows // n_freq
    freq = lax.axis_index("freq")
    for k, out in enumerate(outs):
        block = sums[pl.ds((freq ^ k) * share, share), 8 : 8 + out.shape[2], :]
        out[0] = block.astype(jnp.bfloat16)


def channelize(x, taps, dft, gain, per_frame, n_freq):
    rows = dft.shape[0]
    lanes = TAPS * per_frame
    depth = SAMPLES // TAPS * (lanes // LANES)
    slots, pieces = 3, 4
    return pl.pallas_call(
        functools.partial(channelize_kernel, rows, n_freq),
        in_specs=[pl.BlockSpec(memory_space=pltpu.HBM)] * 4,
        out_specs=[pl.BlockSpec(memory_space=pltpu.VMEM)] * n_freq,
        out_shape=[jax.ShapeDtypeStruct((1, rows // n_freq, depth, LANES), jnp.bfloat16)] * n_freq,
        scratch_shapes=[
            pltpu.VMEM((slots, lanes, NFFT), jnp.int32),
            pltpu.VMEM((TAPS * rows, NFFT), jnp.bfloat16),
            pltpu.VMEM(taps.shape, jnp.float32),
            pltpu.VMEM(dft.shape, jnp.float32),
            pltpu.VMEM(gain.shape, jnp.float32),
            pltpu.VMEM((rows, lanes), jnp.float32),
            pltpu.VMEM((rows, LANES), jnp.float32),
            pltpu.VMEM((rows, depth + 8, LANES), jnp.float32),
            pltpu.SemaphoreType.DMA((slots, pieces)),
            pltpu.SemaphoreType.DMA((3,)),
        ],
        compiler_params=pltpu.CompilerParams(vmem_limit_bytes=VMEM_LIMIT),
        cost_estimate=pl.CostEstimate(
            flops=2 * x.shape[0] * NFFT * TAPS * rows,
            bytes_accessed=x.shape[0] * NFFT * 4,
            transcendentals=0,
        ),
        name="channelize",
    )(x, *[pltpu.with_memory_space_constraint(a, pltpu.HBM) for a in (taps, dft, gain)])


def columns(held, c, first, second, deep):
    half = LANES // 2
    rows = []
    for part in range(2):
        even, odd = held[first, c, part], held[second, c, part]
        rows.append(jnp.concatenate([even[:, :half], odd[:, :half]], axis=1))
        rows.append(jnp.concatenate([even[:, half:], odd[:, half:]], axis=1))
    used = sum(r.shape[0] for r in rows)
    if used < deep:
        rows.append(jnp.zeros((deep - used, LANES), rows[0].dtype))
    return jnp.concatenate(rows, axis=0)


def correlate_kernel(begins, blocks, *refs):
    if begins:
        refs, (out_hbm, lhs_ref, staged, sem) = refs[: len(blocks)], refs[len(blocks) :]
    else:
        lhs_ref, _, *refs, out_hbm, staged, sem = refs
    ch_dev, double, deep = lhs_ref.shape
    width = double // 2
    half = 2 * refs[0].shape[3]
    size = refs[0].shape[0]
    span = size // 2 * LANES
    freq, pair = lax.axis_index("freq"), lax.axis_index("pair")
    copies = []

    def tile(ref, group, c, k):
        flip = freq & (size - 1)
        return columns(ref, c, (2 * k) ^ flip, (2 * k + 1) ^ flip, deep)

    def place(group):
        return pl.multiple_of(((freq // size) ^ group) * span, span)

    for c in range(ch_dev):
        if begins:
            for ref, (slot, group) in zip(refs, blocks):
                if slot:
                    continue
                for k in range(size // 2):
                    own = tile(ref, group, c, k)
                    at = pl.multiple_of(place(group) + k * LANES, LANES)
                    lhs_ref[c, pl.ds(at, LANES), :] = own.T
                    swapped = [own[half : 2 * half], -own[0:half]]
                    if deep > 2 * half:
                        swapped.append(own[2 * half :])
                    swapped = jnp.concatenate(swapped, axis=0).T
                    lhs_ref[c, pl.ds(width + at, LANES), :] = swapped
        for n, (ref, (slot, group)) in enumerate(zip(refs, blocks)):
            rhs = jnp.concatenate([tile(ref, group, c, k) for k in range(size // 2)], axis=1)
            stage = staged.at[c * len(blocks) + n]
            for part in range(2):
                result = jnp.dot(
                    lhs_ref[c, part * width : (part + 1) * width],
                    rhs,
                    preferred_element_type=jnp.float32,
                )
                stage[part] = (result * (1.0 / SAMPLES)).astype(jnp.bfloat16)
            column = pl.multiple_of((pair ^ slot) * width + place(group), span)
            copy = pltpu.make_async_copy(
                stage, out_hbm.at[c, :, :, pl.ds(column, span)], sem.at[c * len(blocks) + n]
            )
            copy.start()
            copies.append(copy)
    for copy in copies:
        copy.wait()


def correlate(lhs, out, held, n_freq, n_pair, per_frame):
    blocks, arrays = list(held), list(held.values())
    _, ch_dev, _, depth, _ = arrays[0].shape
    width = n_freq * per_frame
    deep = -(-4 * depth // LANES) * LANES
    begins = lhs is None
    places = ch_dev * len(blocks)
    whole = pl.BlockSpec(memory_space=pltpu.VMEM)
    there = pl.BlockSpec(memory_space=pl.ANY)
    out_shape = jax.ShapeDtypeStruct((ch_dev, 2, width, n_pair * width), jnp.bfloat16)
    lhs_shape = jax.ShapeDtypeStruct((ch_dev, 2 * width, deep), jnp.bfloat16)
    first = [] if begins else [whole, there]
    return pl.pallas_call(
        functools.partial(correlate_kernel, begins, blocks),
        in_specs=first + [whole] * len(blocks),
        out_specs=[there, whole] if begins else there,
        out_shape=[out_shape, lhs_shape] if begins else out_shape,
        scratch_shapes=[
            pltpu.VMEM((places, 2, width, width // 2), jnp.bfloat16),
            pltpu.SemaphoreType.DMA((places,)),
        ],
        input_output_aliases={} if begins else {1: 0},
        compiler_params=pltpu.CompilerParams(vmem_limit_bytes=VMEM_LIMIT),
        cost_estimate=pl.CostEstimate(flops=0, bytes_accessed=0, transcendentals=0),
        name="correlate",
    )(*([] if begins else [lhs, out]), *arrays)


def correlate_plain(held, per_frame):
    freq, pair = lax.axis_index("freq"), lax.axis_index("pair")
    n_freq, n_pair = lax.axis_size("freq"), lax.axis_size("pair")
    size = n_freq // 2
    _, ch_dev, _, depth, _ = held[0, 0].shape
    share = LANES // per_frame
    order = jnp.arange(size) ^ (freq & (size - 1))
    sides = [jnp.stack([held[slot, 0][order], held[slot, 1][order]]) for slot in range(n_pair)]
    blocks = jnp.stack(sides)[jnp.arange(n_pair) ^ pair][:, jnp.arange(2) ^ (freq // size)]

    def matrix(array):
        array = array.reshape(-1, n_freq, ch_dev, 2, depth, share, per_frame)
        return array.transpose(2, 3, 4, 5, 0, 1, 6).reshape(ch_dev, 2, depth * share, -1)

    row, col = matrix(lax.dynamic_index_in_dim(blocks, pair, 0)), matrix(blocks)

    def contract(a, b):
        return jnp.einsum("csr,csk->crk", a, b, preferred_element_type=jnp.float32)

    real = contract(row[:, 0], col[:, 0]) + contract(row[:, 1], col[:, 1])
    imag = contract(row[:, 1], col[:, 0]) - contract(row[:, 0], col[:, 1])
    return (jnp.stack([real, imag], axis=1) * (1.0 / SAMPLES)).astype(jnp.bfloat16)


def exchange(array, mask):
    size = lax.axis_size("pair")
    return lax.ppermute(array, "pair", [(i, i ^ mask) for i in range(size)])


def body(voltages, gains):
    n_freq, n_pair = lax.axis_size("freq"), lax.axis_size("pair")
    per_frame, frames, _ = voltages.shape
    channels = gains.shape[1]
    ch_dev, size = channels // n_freq, n_freq // 2
    taps, dft = [jnp.asarray(table) for table in tables(channels)]
    x = voltages.transpose(1, 0, 2).reshape(frames * per_frame, NFFT)
    spectra = channelize(x, taps, dft, gains.T, per_frame, n_freq)
    spectra = [a.reshape(1, ch_dev, 2, -1, LANES) for a in spectra]
    spectra = spectra[:1] + [
        lax.ppermute(a, "freq", [(f, f ^ k) for f in range(n_freq)])
        for k, a in enumerate(spectra)
        if k
    ]
    first = jnp.concatenate(spectra[: size // 2])
    second = jnp.concatenate(spectra[size // 2 : size + 1])
    near, far = jnp.concatenate(spectra[:size]), spectra[size:]
    across = [exchange(first, 2), exchange(second, 2)]
    far[1:], across[0] = lax.optimization_barrier((far[1:], across[0]))
    last = exchange(jnp.concatenate(far[1:]), 2)
    far = jnp.concatenate(far)
    held = {(0, 0): near, (1, 0): exchange(near, 1), (0, 1): far, (1, 1): exchange(far, 1)}
    held[2, 0] = jnp.concatenate([across[0], across[1][: size // 2]])
    held[3, 0] = exchange(held[2, 0], 1)
    early = across[1][size // 2 :]
    if n_freq != 8 or 2 * per_frame != LANES or near.shape[3] % 16:
        held[2, 1] = jnp.concatenate([early, last])
        held[3, 1] = exchange(held[2, 1], 1)
        return correlate_plain(held, per_frame)

    def part(lhs, out, *which):
        return correlate(lhs, out, {w: held[w] for w in which}, n_freq, n_pair, per_frame)

    out, lhs = part(None, None, (0, 0), (0, 1), (1, 0), (2, 0), (3, 0), (1, 1))
    last, out = lax.optimization_barrier((last, out))
    held[2, 1] = jnp.concatenate([early, last])
    held[3, 1] = exchange(held[2, 1], 1)
    return part(lhs, out, (2, 1), (3, 1))


def solution(mesh):
    placed = (P(("pair", "freq"), None, None), P(("pair", "freq"), None))
    return jax.shard_map(
        body, mesh=mesh, in_specs=placed, out_specs=P("freq", None, "pair", None), check_vma=False
    )
```

time: 312 us -> 52 us (0.17)
  other arithmetic: 176 us -> 0.17 us
  matrix products: 63.2 us -> 0 us
  blocking collectives: 27.2 us -> 0 us
  Pallas kernels: 0 us -> 25.4 us
  starting transfers between devices: 0.01 us -> 16.5 us
  waiting for transfers between devices: 23.3 us -> 9.66 us
  between operations: 13.5 us -> 0.14 us
  local copies, waits for them, and re-layouts: 9.09 us -> 0.07 us
    convert_element_type x4 -> x0, other arithmetic: 175 us -> none  [the longest x1 131 us: body(): filtered.astype(jnp.bfloat16).reshape(local_inputs * SAMPLES, NFFT)]
    dot_general x5 -> x0, matrix products: 63.2 us -> none  [the longest x1 41 us: body(): lax.dot_general(dft_rows, filtered, (((1,), (1,)), ((), ())), preferred_e...]
    all_to_all x1 -> x0, blocking collectives: 27.2 us -> none  [body(): lax.all_to_all(spectra, 'freq', split_axis=0, concat_axis=1, tiled=True)]
    pallas_call x0 -> x3, Pallas kernels: none -> 25.4 us  [the longest x1 18.8 us: channelize(): pl.pallas_call(functools.partial(channelize_kernel, rows, n_freq), in_spe...]
    all_gather x1 -> x0, waiting for transfers between devices: 23.3 us -> none  [body(): lax.all_gather(row_side, 'pair', axis=3, tiled=True)]
    ppermute x0 -> x14, starting transfers between devices: none -> 16.5 us  [the longest x7 12.5 us: body(): lax.ppermute(a, 'freq', [(f, f ^ k) for f in range(n_freq)])]
    ppermute x0 -> x14, waiting for transfers between devices: none -> 9.66 us  [the longest x7 4.88 us: body(): lax.ppermute(a, 'freq', [(f, f ^ k) for f in range(n_freq)])]
    convert_element_type x2 -> x0, local copies, waits for them, and re-layouts: 5.28 us -> none  [the longest x1 5.08 us: correlate(): return (result * (1.0 / SAMPLES)).astype(jnp.bfloat16)]
  transfers between devices with their start and end apart: 1 -> 14, of which waited for: 1 -> 5; matrix products, arithmetic and copies ran while one was open for 0% -> 0% of each run, Pallas kernels for 0% -> 9%
where the time goes in v1:
time: 52 us; the launch traced here: 51.9 us
  Pallas kernels  25.4 us (49%)
  starting transfers between devices  16.5 us (32%)
  waiting for transfers between devices  9.66 us (19%)
    pallas_call x1, Pallas kernels, channelize(): pl.pallas_call(functools.partial(channelize_kernel, rows, n_freq), in_spe...  18.8 us
    ppermute x7, starting transfers between devices, body(): lax.ppermute(a, 'freq', [(f, f ^ k) for f in range(n_freq)])  12.5 us
    pallas_call x2, Pallas kernels, correlate(): pl.pallas_call(functools.partial(correlate_kernel, begins, blocks), in_sp...  6.62 us
    ppermute x7, waiting for transfers between devices, body(): lax.ppermute(a, 'freq', [(f, f ^ k) for f in range(n_freq)])  4.88 us
    ppermute x7, waiting for transfers between devices, exchange(): return lax.ppermute(array, 'pair', [(i, i ^ mask) for i in range(size)])  4.78 us
    ppermute x7, starting transfers between devices, exchange(): return lax.ppermute(array, 'pair', [(i, i ^ mask) for i in range(size)])  3.94 us
  transfers between devices with their start and end apart: 14, of which 5 were waited for; matrix products, arithmetic and copies ran while one was open for 0% of the time, Pallas kernels for 9%

profile of v1, /device:TPU:0, one launch (start us, length us, event | category | flops | bytes accessed | tf_op | source)
XLA Modules:
  0.0 51.9 jit_solution(8611254607796106598)
XLA Ops:
  0.0 18.8 %channelize.1 = (bf16[1,6,48,128]{3,2,1,0:T(8,128)(2,1)S(1)}, bf16[1,6,48,128]{3,2,1,0:T(8,128)(2,1)S(1)}, bf16[1,6,48,128]{3,2,1,0:T(8,128)(2,1)S(1)}, bf16[1,6...) custom-call(s32[6592,2048]{1,0:T(8,128)} %bitcast.21, ...), custom_call_target="tpu_custom_call" | custom-call | flops 10368319488 | bytes 54001664 | tf_op jit(solution)/shard_map/channelize/pallas_call | solution.py:143
  18.8 3.0 %collective-permute-start = (bf16[1,3,2,48,128]{4,3,2,1,0:T(8,128)(2,1)S(1)}, bf16[1,3,2,48,128]{4,3,2,1,0:T(8,128)(2,1)S(1)}, u32[]{:S(2)}, u32[]{:S(2)}) collective-permute-start(bf16[1,3,2,48,128]{4,3,2,1,0:T(8,128)(2,1)S(1)} %bitcast.20), channel_id=1, source_target_pairs={{0,4},{4,0},{8,12},{12,8},{16,20},{20,16},{24,28},{28,24},{1,5},{5... | collective-permute-start | bytes 221192 | tf_op jit(solution)/shard_map/ppermute | solution.py:304
  21.8 1.6 %collective-permute-start.1 = (bf16[1,3,2,48,128]{4,3,2,1,0:T(8,128)(2,1)S(1)}, bf16[1,3,2,48,128]{4,3,2,1,0:T(8,128)(2,1)S(1)}, u32[]{:S(2)}, u32[]{:S(2)}) collective-permute-start(bf16[1,3,2,48,128]{4,3,2,1,0:T(8,128)(2,1)S(1)} %bitcast.19), channel_id=1, source_target_pairs={{0,8},{4,12},{8,0},{12,4},{16,24},{20,28},{24,16},{28,20},{1,9},{5... | collective-permute-start | bytes 221192 | tf_op jit(solution)/shard_map/ppermute | solution.py:304
  23.3 0.0 collective-permute-start.2
  23.4 3.0 %collective-permute-start.3 = (bf16[1,3,2,48,128]{4,3,2,1,0:T(8,128)(2,1)S(1)}, bf16[1,3,2,48,128]{4,3,2,1,0:T(8,128)(2,1)S(1)}, u32[]{:S(2)}, u32[]{:S(2)}) collective-permute-start(bf16[1,3,2,48,128]{4,3,2,1,0:T(8,128)(2,1)S(1)} %bitcast.17), channel_id=1, source_target_pairs={{0,16},{4,20},{8,24},{12,28},{16,0},{20,4},{24,8},{28,12},{1,17},{... | collective-permute-start | bytes 221192 | tf_op jit(solution)/shard_map/ppermute | solution.py:304
  26.4 1.3 %collective-permute-start.4 = (bf16[1,3,2,48,128]{4,3,2,1,0:T(8,128)(2,1)S(1)}, bf16[1,3,2,48,128]{4,3,2,1,0:T(8,128)(2,1)S(1)}, u32[]{:S(2)}, u32[]{:S(2)}) collective-permute-start(bf16[1,3,2,48,128]{4,3,2,1,0:T(8,128)(2,1)S(1)} %bitcast.16), channel_id=1, source_target_pairs={{0,20},{4,16},{8,28},{12,24},{16,4},{20,0},{24,12},{28,8},{1,21},{... | collective-permute-start | bytes 221192 | tf_op jit(solution)/shard_map/ppermute | solution.py:304
  27.6 0.0 collective-permute-done
  27.6 3.6 %collective-permute-start.5 = (bf16[1,3,2,48,128]{4,3,2,1,0:T(8,128)(2,1)S(1)}, bf16[1,3,2,48,128]{4,3,2,1,0:T(8,128)(2,1)S(1)}, u32[]{:S(2)}, u32[]{:S(2)}) collective-permute-start(bf16[1,3,2,48,128]{4,3,2,1,0:T(8,128)(2,1)S(1)} %bitcast.15), channel_id=1, source_target_pairs={{0,24},{4,28},{8,16},{12,20},{16,8},{20,12},{24,0},{28,4},{1,25},{... | collective-permute-start | bytes 221192 | tf_op jit(solution)/shard_map/ppermute | solution.py:304
  31.3 0.0 collective-permute-done.1
  31.3 0.1 collective-permute-start.6
  31.3 0.0 collective-permute-done.2
  31.4 1.7 %collective-permute-start.7 = (bf16[2,3,2,48,128]{4,3,2,1,0:T(8,128)(2,1)S(1)}, bf16[2,3,2,48,128]{4,3,2,1,0:T(8,128)(2,1)S(1)}, u32[]{:S(2)}, u32[]{:S(2)}) collective-permute-start(bf16[2,3,2,48,128]{4,3,2,1,0:T(8,128)(2,1)S(1)} %pad_maximum_fusion.5), channel_id=1, source_target_pairs={{0,2},{1,3},{2,0},{3,1},{4,6},{5,7},{6,4},{7,5},{8,10},{9,11},{10,... | collective-permute-start | bytes 442376 | tf_op jit(solution)/shard_map/ppermute | solution.py:291
  33.0 0.0 collective-permute-done.3
  33.1 0.5 collective-permute-start.9
  33.6 4.0 %collective-permute-done.4 = bf16[1,3,2,48,128]{4,3,2,1,0:T(8,128)(2,1)S(1)} collective-permute-done((bf16[1,3,2,48,128]{4,3,2,1,0:T(8,128)(2,1)S(1)}, bf16[1,3,2,48,128]{4,3,2,1,0:T(8,128)(2,1)S(1)}, u32[]{:S(2)}, u32[]{:S(2)}) %collective-permute-start.4) | collective-permute-done | bytes 73760 | tf_op jit(solution)/shard_map/ppermute | solution.py:304
  37.6 0.0 collective-permute-start.8
  37.6 0.0 collective-permute-done.5
  37.6 0.9 %collective-permute-done.6 = bf16[1,3,2,48,128]{4,3,2,1,0:T(8,128)(2,1)S(1)} collective-permute-done((bf16[1,3,2,48,128]{4,3,2,1,0:T(8,128)(2,1)S(1)}, bf16[1,3,2,48,128]{4,3,2,1,0:T(8,128)(2,1)S(1)}, u32[]{:S(2)}, u32[]{:S(2)}) %collective-permute-start.6) | collective-permute-done | bytes 73760 | tf_op jit(solution)/shard_map/ppermute | solution.py:304
  38.5 0.0 collective-permute-done.7
  38.5 0.1 collective-permute-start.11
  38.6 1.5 %collective-permute-done.9 = bf16[3,3,2,48,128]{4,3,2,1,0:T(8,128)(2,1)S(1)} collective-permute-done((bf16[3,3,2,48,128]{4,3,2,1,0:T(8,128)(2,1)S(1)}, bf16[3,3,2,48,128]{4,3,2,1,0:T(8,128)(2,1)S(1)}, u32[]{:S(2)}, u32[]{:S(2)}) %collective-permute-start.9) | collective-permute-done | bytes 221216 | tf_op jit(solution)/shard_map/ppermute | solution.py:291
  40.1 0.1 collective-permute-start.10
  40.2 1.6 %collective-permute-start.12 = (bf16[3,3,2,48,128]{4,3,2,1,0:T(8,128)(2,1)S(1)}, bf16[3,3,2,48,128]{4,3,2,1,0:T(8,128)(2,1)S(1)}, u32[]{:S(2)}, u32[]{:S(2)}) collective-permute-start(bf16[3,3,2,48,128]{4,3,2,1,0:T(8,128)(2,1)S(1)} %pad_maximum_fusion.4), channel_id=1, source_target_pairs={{0,2},{1,3},{2,0},{3,1},{4,6},{5,7},{6,4},{7,5},{8,10},{9,11},{10,... | collective-permute-start | bytes 663560 | tf_op jit(solution)/shard_map/ppermute | solution.py:291
  41.8 0.0 collective-permute-done.8.refs_2_
  41.8 0.0 collective-permute-done.11.refs_5_
  41.8 0.0 collective-permute-done.10.refs_4_
  41.9 4.5 %correlate.2 = (bf16[3,2,512,2048]{3,2,1,0:T(8,128)(2,1)}, bf16[3,1024,256]{2,1,0:T(8,128)(2,1)S(1)}) custom-call(bf16[4,3,2,48,128]{4,3,2,1,0:T(8,128)(2,1)S(1)} %pad_maximum_fusion.refs_0_, bf16[4,3,2,48,128]{4,3,2,1,0:T(8,128)(2,1)S(1)} %constant_dynamic-update-slice_fusion.refs_1_, bf16[4,3,2,48,128]{4,3,2,1,0:T(8,128)(2,1)S(1)} %collective-permute-done.8.refs_2_, ...), custom_call_target="tpu_custom_call" | custom-call | tf_op jit(solution)/shard_map/correlate/pallas_call | solution.py:249
  46.4 1.7 %collective-permute-done.12 = bf16[3,3,2,48,128]{4,3,2,1,0:T(8,128)(2,1)S(1)} collective-permute-done((bf16[3,3,2,48,128]{4,3,2,1,0:T(8,128)(2,1)S(1)}, bf16[3,3,2,48,128]{4,3,2,1,0:T(8,128)(2,1)S(1)}, u32[]{:S(2)}, u32[]{:S(2)}) %collective-permute-start.12) | collective-permute-done | bytes 221216 | tf_op jit(solution)/shard_map/ppermute | solution.py:291
  48.2 0.1 collective-permute-start.13
  48.2 1.6 %collective-permute-done.13.refs_3_ = bf16[4,3,2,48,128]{4,3,2,1,0:T(8,128)(2,1)S(1)} collective-permute-done((bf16[4,3,2,48,128]{4,3,2,1,0:T(8,128)(2,1)S(1)}, bf16[4,3,2,48,128]{4,3,2,1,0:T(8,128)(2,1)S(1)}, u32[]{:S(2)}, u32[]{:S(2)}) %collective-permute-start.13) | collective-permute-done | bytes 294944 | tf_op jit(solution)/shard_map/ppermute | solution.py:291
  49.8 2.1 %correlate.3 = bf16[3,2,512,2048]{3,2,1,0:T(8,128)(2,1)} custom-call(bf16[3,1024,256]{2,1,0:T(8,128)(2,1)S(1)} %get-tuple-element.33.refs_0_, bf16[3,2,512,2048]{3,2,1,0:T(8,128)(2,1)} %get-tuple-element.35.refs_1_, bf16[4,3,2,48,128]{4,3,2,1,0:T(8,128)(2,1)S(1)} %pad_maximum_fusion.2.refs_2_, ...), custom_call_target="tpu_custom_call", output_to_operand_aliasing={{}: (1, {})} | custom-call | tf_op jit(solution)/shard_map/correlate/pallas_call | solution.py:249
  (12 shorter events, 0.2 us)
Async XLA Ops:
  18.8 8.9 %collective-permute-start = (bf16[1,3,2,48,128]{4,3,2,1,0:T(8,128)(2,1)S(1)}, bf16[1,3,2,48,128]{4,3,2,1,0:T(8,128)(2,1)S(1)}, u32[]{:S(2)}, u32[]{:S(2)}) collective-permute-start(bf16[1,3,2,48,128]{4,3,2,1,0:T(8,128)(2,1)S(1)} %bitcast.20), channel_id=1, source_target_pairs={{0,4},{4,0},{8,12},{12,8},{16,20},{20,16},{24,28},{28,24},{1,5},{5... | collective-permute-start | bytes 221192 | tf_op jit(solution)/shard_map/ppermute | solution.py:304
  21.8 9.5 %collective-permute-start.1 = (bf16[1,3,2,48,128]{4,3,2,1,0:T(8,128)(2,1)S(1)}, bf16[1,3,2,48,128]{4,3,2,1,0:T(8,128)(2,1)S(1)}, u32[]{:S(2)}, u32[]{:S(2)}) collective-permute-start(bf16[1,3,2,48,128]{4,3,2,1,0:T(8,128)(2,1)S(1)} %bitcast.19), channel_id=1, source_target_pairs={{0,8},{4,12},{8,0},{12,4},{16,24},{20,28},{24,16},{28,20},{1,9},{5... | collective-permute-start | bytes 221192 | tf_op jit(solution)/shard_map/ppermute | solution.py:304
  23.3 8.0 %collective-permute-start.2 = (bf16[1,3,2,48,128]{4,3,2,1,0:T(8,128)(2,1)S(1)}, bf16[1,3,2,48,128]{4,3,2,1,0:T(8,128)(2,1)S(1)}, u32[]{:S(2)}, u32[]{:S(2)}) collective-permute-start(bf16[1,3,2,48,128]{4,3,2,1,0:T(8,128)(2,1)S(1)} %bitcast.18), channel_id=1, source_target_pairs={{0,12},{4,8},{8,4},{12,0},{16,28},{20,24},{24,20},{28,16},{1,13},{... | collective-permute-start | bytes 221192 | tf_op jit(solution)/shard_map/ppermute | solution.py:304
  23.4 9.7 %collective-permute-start.3 = (bf16[1,3,2,48,128]{4,3,2,1,0:T(8,128)(2,1)S(1)}, bf16[1,3,2,48,128]{4,3,2,1,0:T(8,128)(2,1)S(1)}, u32[]{:S(2)}, u32[]{:S(2)}) collective-permute-start(bf16[1,3,2,48,128]{4,3,2,1,0:T(8,128)(2,1)S(1)} %bitcast.17), channel_id=1, source_target_pairs={{0,16},{4,20},{8,24},{12,28},{16,0},{20,4},{24,8},{28,12},{1,17},{... | collective-permute-start | bytes 221192 | tf_op jit(solution)/shard_map/ppermute | solution.py:304
  26.4 11.3 %collective-permute-start.4 = (bf16[1,3,2,48,128]{4,3,2,1,0:T(8,128)(2,1)S(1)}, bf16[1,3,2,48,128]{4,3,2,1,0:T(8,128)(2,1)S(1)}, u32[]{:S(2)}, u32[]{:S(2)}) collective-permute-start(bf16[1,3,2,48,128]{4,3,2,1,0:T(8,128)(2,1)S(1)} %bitcast.16), channel_id=1, source_target_pairs={{0,20},{4,16},{8,28},{12,24},{16,4},{20,0},{24,12},{28,8},{1,21},{... | collective-permute-start | bytes 221192 | tf_op jit(solution)/shard_map/ppermute | solution.py:304
  27.6 10.0 %collective-permute-start.5 = (bf16[1,3,2,48,128]{4,3,2,1,0:T(8,128)(2,1)S(1)}, bf16[1,3,2,48,128]{4,3,2,1,0:T(8,128)(2,1)S(1)}, u32[]{:S(2)}, u32[]{:S(2)}) collective-permute-start(bf16[1,3,2,48,128]{4,3,2,1,0:T(8,128)(2,1)S(1)} %bitcast.15), channel_id=1, source_target_pairs={{0,24},{4,28},{8,16},{12,20},{16,8},{20,12},{24,0},{28,4},{1,25},{... | collective-permute-start | bytes 221192 | tf_op jit(solution)/shard_map/ppermute | solution.py:304
  31.3 7.2 %collective-permute-start.6 = (bf16[1,3,2,48,128]{4,3,2,1,0:T(8,128)(2,1)S(1)}, bf16[1,3,2,48,128]{4,3,2,1,0:T(8,128)(2,1)S(1)}, u32[]{:S(2)}, u32[]{:S(2)}) collective-permute-start(bf16[1,3,2,48,128]{4,3,2,1,0:T(8,128)(2,1)S(1)} %bitcast.14), channel_id=1, source_target_pairs={{0,28},{4,24},{8,20},{12,16},{16,12},{20,8},{24,4},{28,0},{1,29},{... | collective-permute-start | bytes 221192 | tf_op jit(solution)/shard_map/ppermute | solution.py:304
  31.4 7.1 %collective-permute-start.7 = (bf16[2,3,2,48,128]{4,3,2,1,0:T(8,128)(2,1)S(1)}, bf16[2,3,2,48,128]{4,3,2,1,0:T(8,128)(2,1)S(1)}, u32[]{:S(2)}, u32[]{:S(2)}) collective-permute-start(bf16[2,3,2,48,128]{4,3,2,1,0:T(8,128)(2,1)S(1)} %pad_maximum_fusion.5), channel_id=1, source_target_pairs={{0,2},{1,3},{2,0},{3,1},{4,6},{5,7},{6,4},{7,5},{8,10},{9,11},{10,... | collective-permute-start | bytes 442376 | tf_op jit(solution)/shard_map/ppermute | solution.py:291
  33.1 7.0 %collective-permute-start.9 = (bf16[3,3,2,48,128]{4,3,2,1,0:T(8,128)(2,1)S(1)}, bf16[3,3,2,48,128]{4,3,2,1,0:T(8,128)(2,1)S(1)}, u32[]{:S(2)}, u32[]{:S(2)}) collective-permute-start(bf16[3,3,2,48,128]{4,3,2,1,0:T(8,128)(2,1)S(1)} %pad_maximum_fusion.3), channel_id=1, source_target_pairs={{0,2},{1,3},{2,0},{3,1},{4,6},{5,7},{6,4},{7,5},{8,10},{9,11},{10,... | collective-permute-start | bytes 663560 | tf_op jit(solution)/shard_map/ppermute | solution.py:291
  37.6 4.2 %collective-permute-start.8 = (bf16[4,3,2,48,128]{4,3,2,1,0:T(8,128)(2,1)S(1)}, bf16[4,3,2,48,128]{4,3,2,1,0:T(8,128)(2,1)S(1)}, u32[]{:S(2)}, u32[]{:S(2)}) collective-permute-start(bf16[4,3,2,48,128]{4,3,2,1,0:T(8,128)(2,1)S(1)} %pad_maximum_fusion.refs_0_), channel_id=1, source_target_pairs={{0,1},{1,0},{2,3},{3,2},{4,5},{5,4},{6,7},{7,6},{8,9},{9,8},{10,11... | collective-permute-start | bytes 884744 | tf_op jit(solution)/shard_map/ppermute | solution.py:291
  38.5 3.3 %collective-permute-start.11 = (bf16[4,3,2,48,128]{4,3,2,1,0:T(8,128)(2,1)S(1)}, bf16[4,3,2,48,128]{4,3,2,1,0:T(8,128)(2,1)S(1)}, u32[]{:S(2)}, u32[]{:S(2)}) collective-permute-start(bf16[4,3,2,48,128]{4,3,2,1,0:T(8,128)(2,1)S(1)} %constant_dynamic-update-slice_fusion.refs_1_), channel_id=1, source_target_pairs={{0,1},{1,0},{2,3},{3,2},{4,5},{5,4},{6,7},{7,6},{8,9},{9,8},{10,11... | collective-permute-start | bytes 884744 | tf_op jit(solution)/shard_map/ppermute | solution.py:291
  40.1 1.7 %collective-permute-start.10 = (bf16[4,3,2,48,128]{4,3,2,1,0:T(8,128)(2,1)S(1)}, bf16[4,3,2,48,128]{4,3,2,1,0:T(8,128)(2,1)S(1)}, u32[]{:S(2)}, u32[]{:S(2)}) collective-permute-start(bf16[4,3,2,48,128]{4,3,2,1,0:T(8,128)(2,1)S(1)} %pad_maximum_fusion.1.refs_3_), channel_id=1, source_target_pairs={{0,1},{1,0},{2,3},{3,2},{4,5},{5,4},{6,7},{7,6},{8,9},{9,8},{10,11... | collective-permute-start | bytes 884744 | tf_op jit(solution)/shard_map/ppermute | solution.py:291
  40.2 7.9 %collective-permute-start.12 = (bf16[3,3,2,48,128]{4,3,2,1,0:T(8,128)(2,1)S(1)}, bf16[3,3,2,48,128]{4,3,2,1,0:T(8,128)(2,1)S(1)}, u32[]{:S(2)}, u32[]{:S(2)}) collective-permute-start(bf16[3,3,2,48,128]{4,3,2,1,0:T(8,128)(2,1)S(1)} %pad_maximum_fusion.4), channel_id=1, source_target_pairs={{0,2},{1,3},{2,0},{3,1},{4,6},{5,7},{6,4},{7,5},{8,10},{9,11},{10,... | collective-permute-start | bytes 663560 | tf_op jit(solution)/shard_map/ppermute | solution.py:291
  48.2 1.6 %collective-permute-start.13 = (bf16[4,3,2,48,128]{4,3,2,1,0:T(8,128)(2,1)S(1)}, bf16[4,3,2,48,128]{4,3,2,1,0:T(8,128)(2,1)S(1)}, u32[]{:S(2)}, u32[]{:S(2)}) collective-permute-start(bf16[4,3,2,48,128]{4,3,2,1,0:T(8,128)(2,1)S(1)} %pad_maximum_fusion.2.refs_2_), channel_id=1, source_target_pairs={{0,1},{1,0},{2,3},{3,2},{4,5},{5,4},{6,7},{7,6},{8,9},{9,8},{10,11... | collective-permute-start | bytes 884744 | tf_op jit(solution)/shard_map/ppermute | solution.py:291

commit v2 on v1

--- a/solution.py
+++ b/solution.py
@@ -324,10 +324,11 @@
     def part(lhs, out, *which):
         return correlate(lhs, out, {w: held[w] for w in which}, n_freq, n_pair, per_frame)
 
-    out, lhs = part(None, None, (0, 0), (0, 1), (1, 0), (2, 0), (3, 0), (1, 1))
+    out, lhs = part(None, None, (0, 0), (0, 1), (1, 0), (1, 1))
     last, out = lax.optimization_barrier((last, out))
     held[2, 1] = jnp.concatenate([early, last])
     held[3, 1] = exchange(held[2, 1], 1)
+    out = part(lhs, out, (2, 0), (3, 0))
     return part(lhs, out, (2, 1), (3, 1))
 
 

time: 52 us -> 51.6 us (level); the launches traced: 51.9 us -> 50.9 us
  waiting for transfers between devices: 9.66 us -> 7.37 us
  Pallas kernels: 25.4 us -> 26.4 us
    ppermute x7, waiting for transfers between devices: 4.78 us -> 2.49 us  [exchange(): return lax.ppermute(array, 'pair', [(i, i ^ mask) for i in range(size)])]
    pallas_call x2 -> x3, Pallas kernels: 6.62 us -> 7.65 us  [correlate(): pl.pallas_call(functools.partial(correlate_kernel, begins, blocks), in_sp...]
  transfers between devices with their start and end apart: 14 -> 14, of which waited for: 5 -> 3; matrix products, arithmetic and copies ran while one was open for 0% -> 0% of each run, Pallas kernels for 9% -> 11%
where the time goes in v2:
time: 51.6 us; the launch traced here: 50.9 us
  Pallas kernels  26.4 us (51%)
  starting transfers between devices  16.7 us (32%)
  waiting for transfers between devices  7.37 us (14%)
    pallas_call x1, Pallas kernels, channelize(): pl.pallas_call(functools.partial(channelize_kernel, rows, n_freq), in_spe...  18.8 us
    ppermute x7, starting transfers between devices, body(): lax.ppermute(a, 'freq', [(f, f ^ k) for f in range(n_freq)])  12.5 us
    pallas_call x3, Pallas kernels, correlate(): pl.pallas_call(functools.partial(correlate_kernel, begins, blocks), in_sp...  7.65 us
    ppermute x7, waiting for transfers between devices, body(): lax.ppermute(a, 'freq', [(f, f ^ k) for f in range(n_freq)])  4.88 us
    ppermute x7, starting transfers between devices, exchange(): return lax.ppermute(array, 'pair', [(i, i ^ mask) for i in range(size)])  4.17 us
    ppermute x7, waiting for transfers between devices, exchange(): return lax.ppermute(array, 'pair', [(i, i ^ mask) for i in range(size)])  2.49 us
  transfers between devices with their start and end apart: 14, of which 3 were waited for; matrix products, arithmetic and copies ran while one was open for 0% of the time, Pallas kernels for 11%

profile of v2, /device:TPU:0, one launch (start us, length us, event | category | flops | bytes accessed | tf_op | source)
XLA Modules:
  0.0 50.9 jit_solution(3947117740342078500)
XLA Ops:
  0.0 18.8 %channelize.1 = (bf16[1,6,48,128]{3,2,1,0:T(8,128)(2,1)S(1)}, bf16[1,6,48,128]{3,2,1,0:T(8,128)(2,1)S(1)}, bf16[1,6,48,128]{3,2,1,0:T(8,128)(2,1)S(1)}, bf16[1,6...) custom-call(s32[6592,2048]{1,0:T(8,128)} %bitcast.21, ...), custom_call_target="tpu_custom_call" | custom-call | flops 10368319488 | bytes 54001664 | tf_op jit(solution)/shard_map/channelize/pallas_call | solution.py:143
  18.8 3.0 %collective-permute-start = (bf16[1,3,2,48,128]{4,3,2,1,0:T(8,128)(2,1)S(1)}, bf16[1,3,2,48,128]{4,3,2,1,0:T(8,128)(2,1)S(1)}, u32[]{:S(2)}, u32[]{:S(2)}) collective-permute-start(bf16[1,3,2,48,128]{4,3,2,1,0:T(8,128)(2,1)S(1)} %bitcast.20), channel_id=1, source_target_pairs={{0,4},{4,0},{8,12},{12,8},{16,20},{20,16},{24,28},{28,24},{1,5},{5... | collective-permute-start | bytes 221192 | tf_op jit(solution)/shard_map/ppermute | solution.py:304
  21.8 1.6 %collective-permute-start.1 = (bf16[1,3,2,48,128]{4,3,2,1,0:T(8,128)(2,1)S(1)}, bf16[1,3,2,48,128]{4,3,2,1,0:T(8,128)(2,1)S(1)}, u32[]{:S(2)}, u32[]{:S(2)}) collective-permute-start(bf16[1,3,2,48,128]{4,3,2,1,0:T(8,128)(2,1)S(1)} %bitcast.19), channel_id=1, source_target_pairs={{0,8},{4,12},{8,0},{12,4},{16,24},{20,28},{24,16},{28,20},{1,9},{5... | collective-permute-start | bytes 221192 | tf_op jit(solution)/shard_map/ppermute | solution.py:304
  23.3 0.0 collective-permute-start.2
  23.4 3.0 %collective-permute-start.3 = (bf16[1,3,2,48,128]{4,3,2,1,0:T(8,128)(2,1)S(1)}, bf16[1,3,2,48,128]{4,3,2,1,0:T(8,128)(2,1)S(1)}, u32[]{:S(2)}, u32[]{:S(2)}) collective-permute-start(bf16[1,3,2,48,128]{4,3,2,1,0:T(8,128)(2,1)S(1)} %bitcast.17), channel_id=1, source_target_pairs={{0,16},{4,20},{8,24},{12,28},{16,0},{20,4},{24,8},{28,12},{1,17},{... | collective-permute-start | bytes 221192 | tf_op jit(solution)/shard_map/ppermute | solution.py:304
  26.4 1.3 %collective-permute-start.4 = (bf16[1,3,2,48,128]{4,3,2,1,0:T(8,128)(2,1)S(1)}, bf16[1,3,2,48,128]{4,3,2,1,0:T(8,128)(2,1)S(1)}, u32[]{:S(2)}, u32[]{:S(2)}) collective-permute-start(bf16[1,3,2,48,128]{4,3,2,1,0:T(8,128)(2,1)S(1)} %bitcast.16), channel_id=1, source_target_pairs={{0,20},{4,16},{8,28},{12,24},{16,4},{20,0},{24,12},{28,8},{1,21},{... | collective-permute-start | bytes 221192 | tf_op jit(solution)/shard_map/ppermute | solution.py:304
  27.6 0.0 collective-permute-done
  27.6 3.6 %collective-permute-start.5 = (bf16[1,3,2,48,128]{4,3,2,1,0:T(8,128)(2,1)S(1)}, bf16[1,3,2,48,128]{4,3,2,1,0:T(8,128)(2,1)S(1)}, u32[]{:S(2)}, u32[]{:S(2)}) collective-permute-start(bf16[1,3,2,48,128]{4,3,2,1,0:T(8,128)(2,1)S(1)} %bitcast.15), channel_id=1, source_target_pairs={{0,24},{4,28},{8,16},{12,20},{16,8},{20,12},{24,0},{28,4},{1,25},{... | collective-permute-start | bytes 221192 | tf_op jit(solution)/shard_map/ppermute | solution.py:304
  31.3 0.0 collective-permute-done.1
  31.3 0.1 collective-permute-start.6
  31.3 0.0 collective-permute-done.2
  31.4 1.7 %collective-permute-start.7 = (bf16[2,3,2,48,128]{4,3,2,1,0:T(8,128)(2,1)S(1)}, bf16[2,3,2,48,128]{4,3,2,1,0:T(8,128)(2,1)S(1)}, u32[]{:S(2)}, u32[]{:S(2)}) collective-permute-start(bf16[2,3,2,48,128]{4,3,2,1,0:T(8,128)(2,1)S(1)} %pad_maximum_fusion.5), channel_id=1, source_target_pairs={{0,2},{1,3},{2,0},{3,1},{4,6},{5,7},{6,4},{7,5},{8,10},{9,11},{10,... | collective-permute-start | bytes 442376 | tf_op jit(solution)/shard_map/ppermute | solution.py:291
  33.0 0.0 collective-permute-done.3
  33.1 0.5 collective-permute-start.11
  33.6 4.0 %collective-permute-done.4 = bf16[1,3,2,48,128]{4,3,2,1,0:T(8,128)(2,1)S(1)} collective-permute-done((bf16[1,3,2,48,128]{4,3,2,1,0:T(8,128)(2,1)S(1)}, bf16[1,3,2,48,128]{4,3,2,1,0:T(8,128)(2,1)S(1)}, u32[]{:S(2)}, u32[]{:S(2)}) %collective-permute-start.4) | collective-permute-done | bytes 73760 | tf_op jit(solution)/shard_map/ppermute | solution.py:304
  37.6 0.0 collective-permute-start.8
  37.6 0.0 collective-permute-done.5
  37.6 0.9 %collective-permute-done.6 = bf16[1,3,2,48,128]{4,3,2,1,0:T(8,128)(2,1)S(1)} collective-permute-done((bf16[1,3,2,48,128]{4,3,2,1,0:T(8,128)(2,1)S(1)}, bf16[1,3,2,48,128]{4,3,2,1,0:T(8,128)(2,1)S(1)}, u32[]{:S(2)}, u32[]{:S(2)}) %collective-permute-start.6) | collective-permute-done | bytes 73760 | tf_op jit(solution)/shard_map/ppermute | solution.py:304
  38.5 0.0 collective-permute-done.7
  38.5 0.1 collective-permute-start.9
  38.7 1.6 %collective-permute-start.10 = (bf16[3,3,2,48,128]{4,3,2,1,0:T(8,128)(2,1)S(1)}, bf16[3,3,2,48,128]{4,3,2,1,0:T(8,128)(2,1)S(1)}, u32[]{:S(2)}, u32[]{:S(2)}) collective-permute-start(bf16[3,3,2,48,128]{4,3,2,1,0:T(8,128)(2,1)S(1)} %pad_maximum_fusion.3), channel_id=1, source_target_pairs={{0,2},{1,3},{2,0},{3,1},{4,6},{5,7},{6,4},{7,5},{8,10},{9,11},{10,... | collective-permute-start | bytes 663560 | tf_op jit(solution)/shard_map/ppermute | solution.py:291
  40.2 0.0 collective-permute-done.11
  40.3 0.3 collective-permute-start.12
  40.6 0.0 collective-permute-done.8.refs_2_
  40.6 0.0 collective-permute-done.9.refs_3_
  40.6 3.5 %correlate.3 = (bf16[3,2,512,2048]{3,2,1,0:T(8,128)(2,1)}, bf16[3,1024,256]{2,1,0:T(8,128)(2,1)S(1)}) custom-call(bf16[4,3,2,48,128]{4,3,2,1,0:T(8,128)(2,1)S(1)} %pad_maximum_fusion.refs_0_, bf16[4,3,2,48,128]{4,3,2,1,0:T(8,128)(2,1)S(1)} %constant_dynamic-update-slice_fusion.refs_1_, bf16[4,3,2,48,128]{4,3,2,1,0:T(8,128)(2,1)S(1)} %collective-permute-done.8.refs_2_, ...), custom_call_target="tpu_custom_call" | custom-call | tf_op jit(solution)/shard_map/correlate/pallas_call | solution.py:249
  44.1 2.5 %collective-permute-done.10 = bf16[3,3,2,48,128]{4,3,2,1,0:T(8,128)(2,1)S(1)} collective-permute-done((bf16[3,3,2,48,128]{4,3,2,1,0:T(8,128)(2,1)S(1)}, bf16[3,3,2,48,128]{4,3,2,1,0:T(8,128)(2,1)S(1)}, u32[]{:S(2)}, u32[]{:S(2)}) %collective-permute-start.10) | collective-permute-done | bytes 221216 | tf_op jit(solution)/shard_map/ppermute | solution.py:291
  46.6 0.1 collective-permute-start.13
  46.7 0.0 collective-permute-done.12.refs_3_
  46.7 2.1 %correlate.4.refs_1_ = bf16[3,2,512,2048]{3,2,1,0:T(8,128)(2,1)} custom-call(bf16[3,1024,256]{2,1,0:T(8,128)(2,1)S(1)} %get-tuple-element.32.refs_0_, bf16[3,2,512,2048]{3,2,1,0:T(8,128)(2,1)} %get-tuple-element.34.refs_1_, bf16[4,3,2,48,128]{4,3,2,1,0:T(8,128)(2,1)S(1)} %pad_maximum_fusion.1.refs_2_, ...), custom_call_target="tpu_custom_call", output_to_operand_aliasing={{}: (1, {})} | custom-call | tf_op jit(solution)/shard_map/correlate/pallas_call | solution.py:249
  48.8 0.0 collective-permute-done.13.refs_3_
  48.8 2.1 %correlate.5 = bf16[3,2,512,2048]{3,2,1,0:T(8,128)(2,1)} custom-call(bf16[3,1024,256]{2,1,0:T(8,128)(2,1)S(1)} %get-tuple-element.32.refs_0_, bf16[3,2,512,2048]{3,2,1,0:T(8,128)(2,1)} %correlate.4.refs_1_, bf16[4,3,2,48,128]{4,3,2,1,0:T(8,128)(2,1)S(1)} %pad_maximum_fusion.2.refs_2_, ...), custom_call_target="tpu_custom_call", output_to_operand_aliasing={{}: (1, {})} | custom-call | tf_op jit(solution)/shard_map/correlate/pallas_call | solution.py:249
  (12 shorter events, 0.2 us)
Async XLA Ops:
  18.8 8.9 %collective-permute-start = (bf16[1,3,2,48,128]{4,3,2,1,0:T(8,128)(2,1)S(1)}, bf16[1,3,2,48,128]{4,3,2,1,0:T(8,128)(2,1)S(1)}, u32[]{:S(2)}, u32[]{:S(2)}) collective-permute-start(bf16[1,3,2,48,128]{4,3,2,1,0:T(8,128)(2,1)S(1)} %bitcast.20), channel_id=1, source_target_pairs={{0,4},{4,0},{8,12},{12,8},{16,20},{20,16},{24,28},{28,24},{1,5},{5... | collective-permute-start | bytes 221192 | tf_op jit(solution)/shard_map/ppermute | solution.py:304
  21.8 9.5 %collective-permute-start.1 = (bf16[1,3,2,48,128]{4,3,2,1,0:T(8,128)(2,1)S(1)}, bf16[1,3,2,48,128]{4,3,2,1,0:T(8,128)(2,1)S(1)}, u32[]{:S(2)}, u32[]{:S(2)}) collective-permute-start(bf16[1,3,2,48,128]{4,3,2,1,0:T(8,128)(2,1)S(1)} %bitcast.19), channel_id=1, source_target_pairs={{0,8},{4,12},{8,0},{12,4},{16,24},{20,28},{24,16},{28,20},{1,9},{5... | collective-permute-start | bytes 221192 | tf_op jit(solution)/shard_map/ppermute | solution.py:304
  23.3 8.0 %collective-permute-start.2 = (bf16[1,3,2,48,128]{4,3,2,1,0:T(8,128)(2,1)S(1)}, bf16[1,3,2,48,128]{4,3,2,1,0:T(8,128)(2,1)S(1)}, u32[]{:S(2)}, u32[]{:S(2)}) collective-permute-start(bf16[1,3,2,48,128]{4,3,2,1,0:T(8,128)(2,1)S(1)} %bitcast.18), channel_id=1, source_target_pairs={{0,12},{4,8},{8,4},{12,0},{16,28},{20,24},{24,20},{28,16},{1,13},{... | collective-permute-start | bytes 221192 | tf_op jit(solution)/shard_map/ppermute | solution.py:304
  23.4 9.7 %collective-permute-start.3 = (bf16[1,3,2,48,128]{4,3,2,1,0:T(8,128)(2,1)S(1)}, bf16[1,3,2,48,128]{4,3,2,1,0:T(8,128)(2,1)S(1)}, u32[]{:S(2)}, u32[]{:S(2)}) collective-permute-start(bf16[1,3,2,48,128]{4,3,2,1,0:T(8,128)(2,1)S(1)} %bitcast.17), channel_id=1, source_target_pairs={{0,16},{4,20},{8,24},{12,28},{16,0},{20,4},{24,8},{28,12},{1,17},{... | collective-permute-start | bytes 221192 | tf_op jit(solution)/shard_map/ppermute | solution.py:304
  26.4 11.3 %collective-permute-start.4 = (bf16[1,3,2,48,128]{4,3,2,1,0:T(8,128)(2,1)S(1)}, bf16[1,3,2,48,128]{4,3,2,1,0:T(8,128)(2,1)S(1)}, u32[]{:S(2)}, u32[]{:S(2)}) collective-permute-start(bf16[1,3,2,48,128]{4,3,2,1,0:T(8,128)(2,1)S(1)} %bitcast.16), channel_id=1, source_target_pairs={{0,20},{4,16},{8,28},{12,24},{16,4},{20,0},{24,12},{28,8},{1,21},{... | collective-permute-start | bytes 221192 | tf_op jit(solution)/shard_map/ppermute | solution.py:304
  27.6 10.0 %collective-permute-start.5 = (bf16[1,3,2,48,128]{4,3,2,1,0:T(8,128)(2,1)S(1)}, bf16[1,3,2,48,128]{4,3,2,1,0:T(8,128)(2,1)S(1)}, u32[]{:S(2)}, u32[]{:S(2)}) collective-permute-start(bf16[1,3,2,48,128]{4,3,2,1,0:T(8,128)(2,1)S(1)} %bitcast.15), channel_id=1, source_target_pairs={{0,24},{4,28},{8,16},{12,20},{16,8},{20,12},{24,0},{28,4},{1,25},{... | collective-permute-start | bytes 221192 | tf_op jit(solution)/shard_map/ppermute | solution.py:304
  31.3 7.2 %collective-permute-start.6 = (bf16[1,3,2,48,128]{4,3,2,1,0:T(8,128)(2,1)S(1)}, bf16[1,3,2,48,128]{4,3,2,1,0:T(8,128)(2,1)S(1)}, u32[]{:S(2)}, u32[]{:S(2)}) collective-permute-start(bf16[1,3,2,48,128]{4,3,2,1,0:T(8,128)(2,1)S(1)} %bitcast.14), channel_id=1, source_target_pairs={{0,28},{4,24},{8,20},{12,16},{16,12},{20,8},{24,4},{28,0},{1,29},{... | collective-permute-start | bytes 221192 | tf_op jit(solution)/shard_map/ppermute | solution.py:304
  31.4 7.1 %collective-permute-start.7 = (bf16[2,3,2,48,128]{4,3,2,1,0:T(8,128)(2,1)S(1)}, bf16[2,3,2,48,128]{4,3,2,1,0:T(8,128)(2,1)S(1)}, u32[]{:S(2)}, u32[]{:S(2)}) collective-permute-start(bf16[2,3,2,48,128]{4,3,2,1,0:T(8,128)(2,1)S(1)} %pad_maximum_fusion.5), channel_id=1, source_target_pairs={{0,2},{1,3},{2,0},{3,1},{4,6},{5,7},{6,4},{7,5},{8,10},{9,11},{10,... | collective-permute-start | bytes 442376 | tf_op jit(solution)/shard_map/ppermute | solution.py:291
  33.1 7.2 %collective-permute-start.11 = (bf16[3,3,2,48,128]{4,3,2,1,0:T(8,128)(2,1)S(1)}, bf16[3,3,2,48,128]{4,3,2,1,0:T(8,128)(2,1)S(1)}, u32[]{:S(2)}, u32[]{:S(2)}) collective-permute-start(bf16[3,3,2,48,128]{4,3,2,1,0:T(8,128)(2,1)S(1)} %pad_maximum_fusion.4), channel_id=1, source_target_pairs={{0,2},{1,3},{2,0},{3,1},{4,6},{5,7},{6,4},{7,5},{8,10},{9,11},{10,... | collective-permute-start | bytes 663560 | tf_op jit(solution)/shard_map/ppermute | solution.py:291
  37.6 3.0 %collective-permute-start.8 = (bf16[4,3,2,48,128]{4,3,2,1,0:T(8,128)(2,1)S(1)}, bf16[4,3,2,48,128]{4,3,2,1,0:T(8,128)(2,1)S(1)}, u32[]{:S(2)}, u32[]{:S(2)}) collective-permute-start(bf16[4,3,2,48,128]{4,3,2,1,0:T(8,128)(2,1)S(1)} %pad_maximum_fusion.refs_0_), channel_id=1, source_target_pairs={{0,1},{1,0},{2,3},{3,2},{4,5},{5,4},{6,7},{7,6},{8,9},{9,8},{10,11... | collective-permute-start | bytes 884744 | tf_op jit(solution)/shard_map/ppermute | solution.py:291
  38.5 2.1 %collective-permute-start.9 = (bf16[4,3,2,48,128]{4,3,2,1,0:T(8,128)(2,1)S(1)}, bf16[4,3,2,48,128]{4,3,2,1,0:T(8,128)(2,1)S(1)}, u32[]{:S(2)}, u32[]{:S(2)}) collective-permute-start(bf16[4,3,2,48,128]{4,3,2,1,0:T(8,128)(2,1)S(1)} %constant_dynamic-update-slice_fusion.refs_1_), channel_id=1, source_target_pairs={{0,1},{1,0},{2,3},{3,2},{4,5},{5,4},{6,7},{7,6},{8,9},{9,8},{10,11... | collective-permute-start | bytes 884744 | tf_op jit(solution)/shard_map/ppermute | solution.py:291
  38.7 7.9 %collective-permute-start.10 = (bf16[3,3,2,48,128]{4,3,2,1,0:T(8,128)(2,1)S(1)}, bf16[3,3,2,48,128]{4,3,2,1,0:T(8,128)(2,1)S(1)}, u32[]{:S(2)}, u32[]{:S(2)}) collective-permute-start(bf16[3,3,2,48,128]{4,3,2,1,0:T(8,128)(2,1)S(1)} %pad_maximum_fusion.3), channel_id=1, source_target_pairs={{0,2},{1,3},{2,0},{3,1},{4,6},{5,7},{6,4},{7,5},{8,10},{9,11},{10,... | collective-permute-start | bytes 663560 | tf_op jit(solution)/shard_map/ppermute | solution.py:291
  40.3 6.4 %collective-permute-start.12 = (bf16[4,3,2,48,128]{4,3,2,1,0:T(8,128)(2,1)S(1)}, bf16[4,3,2,48,128]{4,3,2,1,0:T(8,128)(2,1)S(1)}, u32[]{:S(2)}, u32[]{:S(2)}) collective-permute-start(bf16[4,3,2,48,128]{4,3,2,1,0:T(8,128)(2,1)S(1)} %pad_maximum_fusion.1.refs_2_), channel_id=1, source_target_pairs={{0,1},{1,0},{2,3},{3,2},{4,5},{5,4},{6,7},{7,6},{8,9},{9,8},{10,11... | collective-permute-start | bytes 884744 | tf_op jit(solution)/shard_map/ppermute | solution.py:291
  46.6 2.2 %collective-permute-start.13 = (bf16[4,3,2,48,128]{4,3,2,1,0:T(8,128)(2,1)S(1)}, bf16[4,3,2,48,128]{4,3,2,1,0:T(8,128)(2,1)S(1)}, u32[]{:S(2)}, u32[]{:S(2)}) collective-permute-start(bf16[4,3,2,48,128]{4,3,2,1,0:T(8,128)(2,1)S(1)} %pad_maximum_fusion.2.refs_2_), channel_id=1, source_target_pairs={{0,1},{1,0},{2,3},{3,2},{4,5},{5,4},{6,7},{7,6},{8,9},{9,8},{10,11... | collective-permute-start | bytes 884744 | tf_op jit(solution)/shard_map/ppermute | solution.py:291
